TPU v7x, 32 devices: a whole 2x2x4 slice. The times are simulated.
32 devices in a mesh: tm: 16 (over z, y, x), tensor: 2 (over core).
Axes of the slice: x: 2, y: 2, z: 4, core: 2. Of those that a mesh axis runs over, the one named last changes fastest.
Arguments:
- query_input: bfloat16 [6144, 2048], P('tm', 'tensor'), may hold values from -6 to 6
- key_input: bfloat16 [6144, 2048], P('tm', 'tensor'), may hold values from -6 to 6
- value_input: bfloat16 [6144, 2048], P('tm', 'tensor'), may hold values from -6 to 6
- log_decay: float32 [16, 6144], P('tensor', 'tm'), may hold values from -0.75 to 0, as said below
- stretch_ids: int32 [6144], P('tm'), may hold values from 0 to 95, as said below
- norm_gain: float32 [2048], P('tensor'), may hold values from 0.1 to 1.9
- out_weight: bfloat16 [2048, 4096], P('tensor'), may hold values from -0.125 to 0.125
- out_cotangent: bfloat16 [6144, 4096], P(('tm', 'tensor')), may hold values from -6 to 6
Outputs:
- layer_out: bfloat16 [6144, 4096], P(('tm', 'tensor'))
- query_grad: bfloat16 [6144, 2048], P('tm', 'tensor')
- key_grad: bfloat16 [6144, 2048], P('tm', 'tensor')
- value_grad: bfloat16 [6144, 2048], P('tm', 'tensor')
Inputs may be any that keep to these rules, and one draw needn't show every extreme that they name: `stretch_ids`: stretch ids never fall along the tokens, start at 0 and rise by at most one at a time, change only at multiples of 32 tokens, and rise at every multiple of 384 tokens, so that no stretch crosses a block; every block holds exactly 6 stretches. `log_decay`: every entry is negative.
All inputs are finite; a program needn't handle non-finite values.
Results may differ from a plain program's by a relative error of at most 0.014.
Values may be sent and summed in bfloat16 or wider, within the bound.
A program may use at most 64 MiB of HBM per device.

v0:
```python
import jax
import jax.numpy as jnp
from jax import lax
from jax.sharding import PartitionSpec as P

EPSILON = 1e-06


def entering(part, axis, combine, identity, reverse):
    count = lax.axis_size(axis)
    place = lax.axis_index(axis)
    ahead = count - 1 - place if reverse else place
    gathered = jax.tree.map(lambda a: lax.all_gather(a, axis), part)
    state = jax.tree.map(lambda a, e: jnp.zeros_like(a) + jnp.asarray(e, a.dtype), part, identity)

    def one(turn, state):
        source = count - 1 - turn if reverse else turn
        return combine(
            state, jax.tree.map(lambda a: lax.dynamic_index_in_dim(a, source, 0, False), gathered)
        )

    return lax.fori_loop(0, ahead, one, state)


def chain_combine(earlier, later):
    return (earlier[0] * later[0], later[0][:, None, None] * earlier[1] + later[1])


def on_device(
    query_input,
    key_input,
    value_input,
    log_decay,
    stretch_ids,
    norm_gain,
    out_weight,
    out_cotangent,
):
    highest = lax.Precision.HIGHEST
    tok_rows = query_input.shape[0]
    heads = log_decay.shape[0]
    head_size = query_input.shape[1] // heads
    query_pos = jnp.maximum(query_input, 0).reshape(tok_rows, heads, head_size)
    key_pos = jnp.maximum(key_input, 0).reshape(tok_rows, heads, head_size)
    value_act = value_input.reshape(tok_rows, heads, head_size)
    cumulative = jnp.cumsum(log_decay, axis=1)
    same_stretch = stretch_ids[:, None] == stretch_ids[None, :]
    visible = stretch_ids[None, :] <= stretch_ids[:, None]
    stretch_end = jnp.min(jnp.where(same_stretch[None], cumulative[:, None, :], jnp.inf), axis=2)
    block_end = cumulative[:, -1]
    weights = jnp.where(
        visible[None],
        jnp.exp(jnp.minimum(stretch_end[:, :, None] - cumulative[:, None, :], 0.0)),
        0.0,
    )
    scores = jnp.einsum("iha,jha->hij", query_pos, key_pos, preferred_element_type=jnp.float32)
    probs = (weights * scores).astype(jnp.bfloat16)
    local_out = jnp.einsum("hij,jhb->ihb", probs, value_act, preferred_element_type=jnp.float32)
    key_scale = jnp.exp(block_end[:, None] - cumulative).T
    decayed = (key_scale[:, :, None] * key_pos).astype(jnp.bfloat16)
    block_state = jnp.einsum("jha,jhb->hab", decayed, value_act, preferred_element_type=jnp.float32)
    block_decay = jnp.exp(block_end)
    identity = (jnp.ones_like(block_decay), jnp.zeros_like(block_state))
    carried_decay, prefix = entering(
        (block_decay, block_state), "tm", chain_combine, identity, False
    )
    end_scale = jnp.exp(stretch_end).T
    carried = jnp.einsum("iha,hab->ihb", query_pos.astype(jnp.float32), prefix, precision=highest)
    mixed = local_out + end_scale[:, :, None] * carried
    inv_rms = lax.rsqrt(jnp.mean(mixed * mixed, axis=2) + EPSILON)
    gain_heads = norm_gain.reshape(heads, head_size)
    attended = (
        (mixed * inv_rms[:, :, None] * gain_heads)
        .astype(jnp.bfloat16)
        .reshape(tok_rows, heads * head_size)
    )
    layer_out = lax.psum_scatter(
        jnp.dot(attended, out_weight, preferred_element_type=jnp.float32).astype(jnp.bfloat16),
        "tensor",
        scatter_dimension=0,
        tiled=True,
    )
    out_grad = lax.dot_general(
        lax.all_gather(out_cotangent, "tensor", axis=0, tiled=True),
        out_weight,
        (((1,), (1,)), ((), ())),
        preferred_element_type=jnp.float32,
    ).reshape(tok_rows, heads, head_size)
    gained = out_grad * gain_heads
    along = jnp.mean(mixed * gained, axis=2)
    cube = inv_rms * inv_rms * inv_rms
    mixed_grad = (inv_rms[:, :, None] * gained - mixed * (cube * along)[:, :, None]).astype(
        jnp.bfloat16
    )
    prob_grad = jnp.einsum(
        "ihb,jhb->hij", mixed_grad, value_act, preferred_element_type=jnp.float32
    )
    score_grad = (weights * prob_grad).astype(jnp.bfloat16)
    value_local = jnp.einsum("hij,ihb->jhb", probs, mixed_grad, preferred_element_type=jnp.float32)
    query_local = jnp.einsum(
        "hij,jha->iha", score_grad, key_pos, preferred_element_type=jnp.float32
    )
    key_local = jnp.einsum(
        "hij,iha->jha", score_grad, query_pos, preferred_element_type=jnp.float32
    )
    scaled_query = (end_scale[:, :, None] * query_pos).astype(jnp.bfloat16)
    state_grad = jnp.einsum(
        "iha,ihb->hab", scaled_query, mixed_grad, preferred_element_type=jnp.float32
    )
    later_decay, later = entering((block_decay, state_grad), "tm", chain_combine, identity, True)
    value_carry = jnp.einsum("jha,hab->jhb", decayed.astype(jnp.float32), later, precision=highest)
    key_carry = key_scale[:, :, None] * jnp.einsum(
        "jhb,hab->jha", value_act.astype(jnp.float32), later, precision=highest
    )
    query_carry = end_scale[:, :, None] * jnp.einsum(
        "ihb,hab->iha", mixed_grad.astype(jnp.float32), prefix, precision=highest
    )
    flat = (tok_rows, heads * head_size)
    query_grad = (
        jnp.where(
            query_input.reshape(tok_rows, heads, head_size) > 0, query_local + query_carry, 0.0
        )
        .astype(jnp.bfloat16)
        .reshape(flat)
    )
    key_grad = (
        jnp.where(key_input.reshape(tok_rows, heads, head_size) > 0, key_local + key_carry, 0.0)
        .astype(jnp.bfloat16)
        .reshape(flat)
    )
    value_grad = (value_local + value_carry).astype(jnp.bfloat16).reshape(flat)
    return (layer_out, query_grad, key_grad, value_grad)


def solution(mesh):
    return jax.shard_map(
        on_device,
        mesh=mesh,
        in_specs=(
            P("tm", "tensor"),
            P("tm", "tensor"),
            P("tm", "tensor"),
            P("tensor", "tm"),
            P("tm"),
            P("tensor"),
            P("tensor", None),
            P(("tm", "tensor"), None),
        ),
        out_specs=(
            P(("tm", "tensor"), None),
            P("tm", "tensor"),
            P("tm", "tensor"),
            P("tm", "tensor"),
        ),
        check_vma=False,
    )
```

profile of v0, /device:TPU:0, one launch (start us, length us, event | category | flops | bytes accessed | tf_op | source)
XLA Modules:
  0.0 313.0 jit_solution(6454433201541228665)
XLA Ops:
  13.0 43.6 %all-reduce = f32[128]{0:T(128)S(1)} all-reduce(f32[128]{0:T(128)S(1)} %dynamic-update-slice), channel_id=2, replica_groups=mesh['tm'=16,'tensor'=2] {'tm'}, use_global_device_ids=true, to_apply=%add | all-reduce | flops 128 | bytes 1024
  58.3 2.8 multiply_convert_fusion.1
  61.2 10.0 %fusion.21 = f32[384,1024]{0,1:T(8,128)} fusion(bf16[384,4096]{1,0:T(8,128)(2,1)} %all-gather.7.cloned.1.call-done, bf16[1024,4096]{1,0:T(8,128)(2,1)} %param.18), kind=kOutput, calls=%fused_computation.54 | convolution fusion | flops 3221225472 | bytes 13107200 | tf_op jit(solution)/shard_map/dot_general | solution.py:83
  71.2 70.7 %all-gather.9.cloned.1.call-done = f32[128,128,128]{2,1,0:T(8,128)} async-done(((f32[8,128,128]{2,1,0:T(8,128)}), f32[128,128,128]{2,1,0:T(8,128)}) %all-gather.9.cloned.1.call-update) | async-done | bytes 8388624 | tf_op jit(solution)/shard_map/all_gather | solution.py:13
  143.7 2.5 multiply_reduce_fusion
  146.2 1.4 subtract_convert_fusion
  147.6 1.3 fusion.7
  149.1 8.9 %convolution_convert_fusion = bf16[384,4096]{1,0:T(8,128)(2,1)} fusion(bf16[384,1024]{0,1:T(8,128)(2,1)} %bitcast.127, bf16[1024,4096]{1,0:T(8,128)(2,1)} %param.18), kind=kOutput, calls=%fused_computation.4 | convolution fusion | flops 3222798336 | bytes 12320768 | tf_op jit(solution)/shard_map/dot_general | solution.py:78
  158.0 1.4 broadcast_compare_fusion
  161.4 1.9 multiply_convert_fusion
  163.3 1.8 fusion.5
  165.1 2.3 copy.95
  167.4 3.5 %fusion.23 = f32[8,128,384]{2,1,0:T(8,128)} fusion(bf16[384,8,128]{0,2,1:T(8,128)(2,1)S(1)} %get-tuple-element.174, bf16[8,384,384]{2,1,0:T(8,128)(2,1)} %multiply_convert_fusion.1), kind=kOutput, calls=%fused_computation.56 | convolution fusion | flops 301989888 | bytes 4718592 | tf_op jit(solution)/shard_map/hij,ihb->jhb/dot_general | solution.py:99
  170.9 107.6 %all-gather.11.cloned.1.call-done = f32[128,128,128]{2,1,0:T(8,128)} async-done(((f32[8,128,128]{2,1,0:T(8,128)}), f32[128,128,128]{2,1,0:T(8,128)}) %all-gather.11.cloned.1.call-update) | async-done | bytes 8388624 | tf_op jit(solution)/shard_map/all_gather | solution.py:13
  278.6 18.9 %while.27 = (s32[]{:T(128)}, f32[8,128,128]{2,1,0:T(8,128)S(1)}, s32[]{:T(128)}, f32[16,8]{1,0:T(8,128)S(1)}, f32[16,8,128,128]{3,2,1,0:T(8,128)}, /*index=5*/s32[]{:T(128)}, s32[]{:T(128)}, s32[]{:T(128)}, s32[]{:T(128)}) while((s32[]{:T(128)}, f32[8,128,128]{2,1,0:T(8,128)S(1)}, s32[]{:T(128)}, f32[16,8]{1,0:T(8,128)S(1)}, ...), condition=%wide.region_9.10_spmd, body=%wide.region_8.9_spmd.sunk | while | flops 262150 | bytes 1573107 | solution.py:22
  278.6 1.3 bitcast_add_fusion.5
  279.9 1.2 bitcast_add_fusion.5
  281.2 1.2 bitcast_add_fusion.5
  282.4 1.2 bitcast_add_fusion.5
  283.6 1.2 bitcast_add_fusion.5
  284.9 1.3 bitcast_add_fusion.5
  286.3 1.2 bitcast_add_fusion.5
  287.5 1.2 bitcast_add_fusion.5
  288.8 1.2 bitcast_add_fusion.5
  290.0 1.2 bitcast_add_fusion.5
  291.3 1.2 bitcast_add_fusion.5
  292.5 1.2 bitcast_add_fusion.5
  293.8 1.2 bitcast_add_fusion.5
  295.0 1.2 bitcast_add_fusion.5
  296.2 1.2 bitcast_add_fusion.5
  297.5 3.2 %add_convert_fusion = bf16[8,128,384]{2,1,0:T(8,128)(2,1)} fusion(f32[8,128,384]{2,1,0:T(8,128)} %fusion.23, f32[8,128,128]{2,1,0:T(8,128)S(1)} %get-tuple-element.133, bf16[384,8,128]{0,2,1:T(8,128)(2,1)S(1)} %bitcast.118, f32[384,8]{0,1:T(8,128)S(1)} %exponential_bitcast_fusion), kind=kOutput, calls=%fused_computation.19 | convolution fusion | flops 605945856 | bytes 3682304 | tf_op jit(solution)/shard_map/jha,hab->jhb/dot_general | solution.py:111
  300.6 2.3 copy.97
  (85 shorter events, 14.4 us)
Async XLA Ops:
  7.2 3.1 copy-start
  7.2 1.2 copy-start.8
  7.2 54.0 %all-gather.7.cloned.1.call-start = ((), (), s32[]{:S(2)}) async-start(), calls=%async_computation.2 | async-start | bytes 4718592 | tf_op jit(solution)/shard_map/all_gather | solution.py:84
  7.9 0.9 copy-start.12
  7.9 134.0 %all-gather.9.cloned.1.call-start = ((), (), s32[]{:S(2)}) async-start(), calls=%async_computation.3 | async-start | bytes 8912896 | tf_op jit(solution)/shard_map/all_gather | solution.py:13
  8.8 49.5 %copy-start.4 = (bf16[384,1024]{0,1:T(8,128)(2,1)}, bf16[384,1024]{0,1:T(8,128)(2,1)S(1)}, u32[]{:S(2)}) copy-start(bf16[384,1024]{0,1:T(8,128)(2,1)S(1)} %copy.78) | copy-start | bytes 2359300
  8.8 2.7 copy-start.14
  8.8 47.9 %copy-start.9 = (bf16[384,1024]{1,0:T(8,128)(2,1)S(1)}, bf16[384,1024]{1,0:T(8,128)(2,1)}, u32[]{:S(2)}) copy-start(bf16[384,1024]{1,0:T(8,128)(2,1)} %param.12) | copy-start | bytes 2359300
  11.5 267.1 %all-gather.11.cloned.1.call-start = ((), (), s32[]{:S(2)}) async-start(), calls=%async_computation.4 | async-start | bytes 8912896 | tf_op jit(solution)/shard_map/all_gather | solution.py:13
  56.8 0.7 copy-start.13
  142.0 1.7 copy-start.3
  142.0 1.7 copy-start.11
  143.7 2.5 copy-start.7
  148.9 157.6 %reduce-scatter.2.cloned.1.call-start = ((), (), s32[]{:S(2)}) async-start(), calls=%async_computation.1 | async-start | bytes 4718592 | tf_op jit(solution)/shard_map/reduce_scatter | solution.py:77
  158.0 1.9 copy-start.10
  161.4 1.9 copy-start.5
  163.3 1.8 copy-start.1
  278.6 18.9 %copy-start.6 = (bf16[384,1024]{0,1:T(8,128)(2,1)S(1)}, bf16[384,1024]{0,1:T(8,128)(2,1)}, u32[]{:S(2)}) copy-start(bf16[384,1024]{0,1:T(8,128)(2,1)} %copy-done.4) | copy-start | bytes 2359300
  302.9 1.7 copy-start.2
Sparse Core Ops, SparseCore 0:
  9.6 14.8 all-gather.6
  27.8 114.1 all-gather.8
  149.0 129.4 all-gather.10
  281.2 9.0 reduce-scatter.1
where the time goes:
time: 314 us; the launch traced here: 313 us
  waiting for transfers between devices  179 us (57%)
  blocking collectives  43.6 us (14%)
  matrix products  40.4 us (13%)
  other arithmetic  23.2 us (7%)
  between operations  14.7 us (5%)
  local copies, waits for them, and re-layouts  11 us (4%)
    all_gather x2, waiting for transfers between devices, entering(): gathered = jax.tree.map(lambda a: lax.all_gather(a, axis), part)  178 us
    unnamed x1, blocking collectives  43.6 us
    add x15, other arithmetic, chain_combine(): later[0][:, None, None] * earlier[1] + later[1]  18.2 us
    dot_general x1, matrix products, on_device(): lax.dot_general(lax.all_gather(out_cotangent, 'tensor', axis=0, tiled=Tru...  10 us
    dot_general x1, matrix products, on_device(): jnp.dot(attended, out_weight, preferred_element_type=jnp.float32)  8.85 us
    unnamed x36, local copies, waits for them, and re-layouts  8.7 us
  transfers between devices with their start and end apart: 4, of which 2 were waited for; matrix products, arithmetic and copies ran while one was open for 21% of the time, Pallas kernels for 0%

commit v1 on v0

v1 whole, which is shorter than its diff:
```python
import functools

import jax
import jax.numpy as jnp
from jax import lax
from jax.experimental import pallas as pl
from jax.experimental.pallas import tpu as pltpu
from jax.sharding import PartitionSpec as P

EPSILON = 1e-06
F32 = jnp.float32
BF16 = jnp.bfloat16
MESH = pl.DeviceIdType.MESH
NT = (((1,), (1,)), ((), ()))
TN = (((0,), (0,)), ((), ()))
NN = (((1,), (0,)), ((), ()))


def mm(a, b, dims, precision=None):
    return lax.dot_general(a, b, dims, precision=precision, preferred_element_type=F32)


def owners_of(rows, head_size, count):
    owners = count
    while rows % owners or (rows // owners) % 16 or head_size % (rows // owners):
        owners -= 1
    return owners


def kernel(
    n, nt, owners,
    q_ref, k_ref, v_ref, ld_ref, sid_ref, gain_ref, w_hbm, cot_hbm,
    out_ref, qg_ref, kg_ref, vg_ref,
    w, cot, bound, cumrow, kscale, escale, decayed, weights, probs, local, outgrad,
    attended, mixgrad, vlocal, klocal, decays,
    send_s, recv_s, send_p, prefix, send_g, recv_g, send_l, later, send_o, recv_o,
    w_sem, cot_sem, c_send, c_recv, s_send, s_recv, p_send, p_recv,
    g_send, g_recv, l_send, l_recv, o_send, o_recv,
):
    me = lax.axis_index("tm")
    my_t = lax.axis_index("tensor")
    tok = q_ref.shape[0]
    heads = ld_ref.shape[0]
    hd = q_ref.shape[1] // heads
    rows_t = tok // nt
    piece = heads * hd // owners
    per_head = owners // heads
    wide = w.shape[1]

    def other(k):
        return lax.rem(me + k, n)

    def source(k):
        return lax.rem(me + n - k, n)

    def owner_only(index, body):
        if owners == n:
            body()
        else:
            pl.when(index < owners)(body)

    def partners(body, lowest=1, count=n):
        def step(k, carry):
            body(k)
            return carry

        lax.fori_loop(lowest, count, step, 0)

    def each_head(body):
        def step(h, carry):
            body(h, pl.ds(pl.multiple_of(h * hd, hd), hd))
            return carry

        lax.fori_loop(0, heads, step, 0)

    barrier = pltpu.get_barrier_semaphore()
    partners(lambda k: pl.semaphore_signal(
        barrier, inc=1, device_id={"tm": other(k)}, device_id_type=MESH))
    partners(lambda k: pl.semaphore_signal(
        barrier, inc=1, device_id={"tensor": lax.rem(my_t + k, nt)}, device_id_type=MESH), 1, nt)

    w_copy = pltpu.make_async_copy(w_hbm, w, w_sem)
    w_copy.start()
    my_rows = pl.ds(pl.multiple_of(my_t * rows_t, 16), rows_t)
    cot_copy = pltpu.make_async_copy(cot_hbm, cot.at[my_rows], cot_sem)
    cot_copy.start()

    row_id = lax.broadcasted_iota(jnp.int32, (tok, tok), 0)
    col_id = lax.broadcasted_iota(jnp.int32, (tok, tok), 1)
    sid = sid_ref[...].astype(F32)
    sid_row = jnp.broadcast_to(sid, (tok, tok))
    sid_col = jnp.sum(jnp.where(row_id == col_id, sid_row, 0.0), axis=1, keepdims=True)
    visible = sid_row <= sid_col
    bound[...] = jnp.where(visible, 0.0, -1e30)
    ld = ld_ref[...]
    highest = lax.Precision.HIGHEST
    tri = jnp.where(col_id <= row_id, 1.0, 0.0)
    cumrow[...] = mm(ld, tri, NT, highest)
    cumcol = mm(tri, ld, NT, highest)
    cendcol = mm(jnp.where(visible, 1.0, 0.0), ld, NT, highest)
    top = lax.broadcasted_iota(jnp.int32, (16, hd), 0) < 8
    for h in range(heads):
        cum_h = cumcol[:, h : h + 1]
        end_h = cum_h[tok - 1 : tok]
        kscale[h] = jnp.broadcast_to(jnp.exp(end_h - cum_h), (tok, hd))
        escale[h] = jnp.broadcast_to(cendcol[:, h : h + 1], (tok, hd))
        g = jnp.broadcast_to(jnp.exp(end_h), (16, hd))
        high = g.astype(BF16).astype(F32)
        extra = jnp.where(top, high, g - high).astype(BF16)
        for r in range(per_head):
            send_s[h * per_head + r, piece:, :] = extra

    def state_step(h, cols):
        kp = jnp.maximum(k_ref[:, cols], 0).astype(F32)
        dec = (kscale[h] * kp).astype(BF16)
        decayed[:, cols] = dec
        state = mm(dec, v_ref[:, cols], TN).astype(BF16)
        for r in range(per_head):
            send_s[h * per_head + r, :piece, :] = state[r * piece : (r + 1) * piece]

    each_head(state_step)
    pl.semaphore_wait(barrier, n - 1 + nt - 1)

    def to_owner(src, dst, ss, rs, k):
        d = other(k)
        return pltpu.make_async_remote_copy(
            src.at[d if owners == n else jnp.minimum(d, owners - 1)], dst.at[me],
            ss.at[k], rs.at[k], device_id={"tm": d}, device_id_type=MESH)

    def from_any(src, dst, ss, rs, k):
        return pltpu.make_async_remote_copy(
            src.at[0], dst.at[source(k)], ss.at[k], rs.at[k],
            device_id={"tm": other(k)}, device_id_type=MESH)

    slot_me = me if owners == n else jnp.minimum(me, owners - 1)

    def to_any(src, dst, ss, rs, k):
        d = other(k)
        return pltpu.make_async_remote_copy(
            src.at[d], dst.at[slot_me], ss.at[k], rs.at[k],
            device_id={"tm": d}, device_id_type=MESH)

    def from_owner(src, dst, ss, rs, k):
        s = source(k)
        return pltpu.make_async_remote_copy(
            src.at[0], dst.at[s if owners == n else jnp.minimum(s, owners - 1)],
            ss.at[k], rs.at[k], device_id={"tm": other(k)}, device_id_type=MESH)

    def gather_start(src, dst, ss, rs):
        partners(lambda k: owner_only(other(k), lambda: to_owner(src, dst, ss, rs, k).start()))

        def keep():
            dst[me] = src[slot_me]

        owner_only(me, keep)

    def gather_wait(src, dst, ss, rs):
        owner_only(me, lambda: partners(lambda k: from_any(src, dst, ss, rs, k).wait_recv()))

    def spread_start(src, dst, ss, rs):
        def go():
            partners(lambda k: to_any(src, dst, ss, rs, k).start())
            dst[slot_me] = src[me]

        owner_only(me, go)

    def spread_wait(src, dst, ss, rs):
        partners(lambda k: owner_only(
            source(k), lambda: from_owner(src, dst, ss, rs, k).wait_recv()))

    def sends_wait(src_g, dst_g, ss_g, rs_g, src_s, dst_s, ss_s, rs_s):
        partners(lambda k: owner_only(
            other(k), lambda: to_owner(src_g, dst_g, ss_g, rs_g, k).wait_send()))
        owner_only(me, lambda: partners(
            lambda k: to_any(src_s, dst_s, ss_s, rs_s, k).wait_send()))

    fwd_g = (send_s, recv_s, s_send, s_recv)
    fwd_s = (send_p, prefix, p_send, p_recv)
    bwd_g = (send_g, recv_g, g_send, g_recv)
    bwd_s = (send_l, later, l_send, l_recv)

    gather_start(*fwd_g)

    def cot_remote(k):
        return pltpu.make_async_remote_copy(
            cot_hbm, cot.at[my_rows], c_send.at[k], c_recv.at[k],
            device_id={"tensor": lax.rem(my_t + k, nt)}, device_id_type=MESH)

    def cot_arrival(k):
        s = lax.rem(my_t + nt - k, nt)
        return pltpu.make_async_remote_copy(
            cot_hbm, cot.at[pl.ds(pl.multiple_of(s * rows_t, 16), rows_t)],
            c_send.at[k], c_recv.at[k],
            device_id={"tensor": lax.rem(my_t + k, nt)}, device_id_type=MESH)

    partners(lambda k: cot_remote(k).start(), 1, nt)

    def inner_step(h, cols):
        qp = jnp.maximum(q_ref[:, cols], 0)
        kp = jnp.maximum(k_ref[:, cols], 0)
        end = jnp.concatenate([escale[h]] * (tok // hd), axis=1)
        weight = jnp.exp(jnp.minimum(end - cumrow[pl.ds(h, 1), :], bound[...]))
        weights[h] = weight
        p = (weight * mm(qp, kp, NT)).astype(BF16)
        probs[h] = p
        local[:, cols] = mm(p, v_ref[:, cols], NN)
        escale[h] = jnp.exp(escale[h])

    each_head(inner_step)

    gather_wait(*fwd_g)

    def scan_forward():
        def step(b, state):
            send_p[b] = state.astype(BF16)
            got = recv_s[b].astype(F32)
            g = got[piece : piece + 1] + got[piece + 8 : piece + 9]
            decays[pl.ds(b, 1), :] = g
            return g * state + got[:piece]

        lax.fori_loop(0, n, step, jnp.zeros((piece, hd), F32))

    owner_only(me, scan_forward)
    spread_start(*fwd_s)

    w_copy.wait()
    cot_copy.wait()
    partners(lambda k: cot_arrival(k).wait_recv(), 1, nt)
    chunk = 2 * hd if heads % 2 == 0 else hd

    def outgrad_step(c, carry):
        part = pl.ds(pl.multiple_of(c * chunk, chunk), chunk)
        outgrad[:, part] = mm(cot[...], w[part, :], NT)
        return carry

    lax.fori_loop(0, heads * hd // chunk, outgrad_step, 0)

    spread_wait(*fwd_s)

    def head_rows(buffer, h):
        parts = [buffer[h * per_head + r] for r in range(per_head)]
        return parts[0] if per_head == 1 else jnp.concatenate(parts, axis=0)

    def norm_step(h, cols):
        qp = jnp.maximum(q_ref[:, cols], 0)
        es = escale[h]
        mixed = local[:, cols] + es * mm(qp, head_rows(prefix, h), NN)
        inv = lax.rsqrt(jnp.mean(mixed * mixed, axis=1, keepdims=True) + EPSILON)
        gain = gain_ref[:, cols]
        attended[:, cols] = (mixed * inv * gain).astype(BF16)
        gained = outgrad[:, cols] * gain
        along = jnp.mean(mixed * gained, axis=1, keepdims=True)
        mg = (inv * gained - mixed * (inv * inv * inv * along)).astype(BF16)
        mixgrad[:, cols] = mg
        sq = (es * qp.astype(F32)).astype(BF16)
        grad = mm(sq, mg, TN).astype(BF16)
        for r in range(per_head):
            send_g[h * per_head + r] = grad[r * piece : (r + 1) * piece]

    each_head(norm_step)
    gather_start(*bwd_g)

    step_cols = 512

    def project(t, sink):
        rows = pl.ds(pl.multiple_of(t * rows_t, 16), rows_t)

        def step(c, carry):
            part = pl.ds(pl.multiple_of(c * step_cols, step_cols), step_cols)
            sink(part, mm(attended[rows, :], w[:, part], NN))
            return carry

        lax.fori_loop(0, wide // step_cols, step, 0)

    def out_copy(k):
        return pltpu.make_async_remote_copy(
            send_o.at[k - 1], recv_o.at[k - 1], o_send.at[k], o_recv.at[k],
            device_id={"tensor": lax.rem(my_t + k, nt)}, device_id_type=MESH)

    for k in range(1, nt):
        def keep_out(part, value, k=k):
            send_o[k - 1, :, part] = value.astype(BF16)

        project(lax.rem(my_t + k, nt), keep_out)
        out_copy(k).start()

    gather_wait(*bwd_g)

    def scan_backward():
        def step(i, state):
            b = n - 1 - i
            send_l[b] = state.astype(BF16)
            return decays[pl.ds(b, 1), :] * state + recv_g[b].astype(F32)

        lax.fori_loop(0, n, step, jnp.zeros((piece, hd), F32))

    owner_only(me, scan_backward)
    spread_start(*bwd_s)

    def grad_step(h, cols):
        qp = jnp.maximum(q_ref[:, cols], 0)
        kp = jnp.maximum(k_ref[:, cols], 0)
        mg = mixgrad[:, cols]
        sg = (weights[h] * mm(mg, v_ref[:, cols], NT)).astype(BF16)
        vlocal[:, cols] = mm(probs[h], mg, TN)
        klocal[:, cols] = mm(sg, qp, TN)
        qg = mm(sg, kp, NN) + escale[h] * mm(mg, head_rows(prefix, h), NT)
        qg_ref[:, cols] = jnp.where(qp.astype(F32) > 0, qg, 0.0).astype(BF16)

    each_head(grad_step)

    for k in range(1, nt):
        out_copy(k).wait_recv()

    def keep_own(part, value):
        total = value.astype(BF16).astype(F32)
        for k in range(1, nt):
            total += recv_o[k - 1, :, part].astype(F32)
        out_ref[:, part] = total.astype(BF16)

    project(my_t, keep_own)

    spread_wait(*bwd_s)

    def last_step(h, cols):
        lat = head_rows(later, h)
        vg_ref[:, cols] = (vlocal[:, cols] + mm(decayed[:, cols], lat, NN)).astype(BF16)
        kg = klocal[:, cols] + kscale[h] * mm(v_ref[:, cols], lat, NT)
        kg_ref[:, cols] = jnp.where(k_ref[:, cols].astype(F32) > 0, kg, 0.0).astype(BF16)

    each_head(last_step)

    partners(lambda k: cot_remote(k).wait_send(), 1, nt)
    for k in range(1, nt):
        out_copy(k).wait_send()
    sends_wait(*fwd_g, *fwd_s)
    sends_wait(*bwd_g, *bwd_s)


def on_device(n, nt, q, k, v, ld, sid, gain, w, cot):
    tok, width = q.shape
    heads = ld.shape[0]
    hd = width // heads
    wide = w.shape[1]
    rows_t = cot.shape[0]
    owners = owners_of(width, hd, n)
    piece = width // owners
    vmem = pl.BlockSpec(memory_space=pltpu.VMEM)
    hbm = pl.BlockSpec(memory_space=pl.ANY)
    dma = pltpu.SemaphoreType.DMA
    flat16 = pltpu.VMEM((tok, width), BF16)
    flat32 = pltpu.VMEM((tok, width), F32)
    cost = pl.CostEstimate(
        flops=4 * tok * width * wide + 14 * tok * tok * width + 12 * tok * width * hd,
        bytes_accessed=2 * width * wide + 16 * tok * width,
        transcendentals=heads * tok * tok,
    )
    return pl.pallas_call(
        functools.partial(kernel, n, nt, owners),
        out_shape=(
            jax.ShapeDtypeStruct((rows_t, wide), BF16),
            jax.ShapeDtypeStruct((tok, width), BF16),
            jax.ShapeDtypeStruct((tok, width), BF16),
            jax.ShapeDtypeStruct((tok, width), BF16),
        ),
        in_specs=[vmem] * 6 + [hbm] * 2,
        out_specs=(vmem,) * 4,
        scratch_shapes=[
            pltpu.VMEM(w.shape, BF16),
            pltpu.VMEM((tok, wide), BF16),
            pltpu.VMEM((tok, tok), F32),
            pltpu.VMEM((heads, tok), F32),
            pltpu.VMEM((heads, tok, hd), F32),
            pltpu.VMEM((heads, tok, hd), F32),
            flat16,
            pltpu.VMEM((heads, tok, tok), F32),
            pltpu.VMEM((heads, tok, tok), BF16),
            flat32, flat32, flat16, flat16, flat32, flat32,
            pltpu.VMEM((n, hd), F32),
            pltpu.VMEM((owners, piece + 16, hd), BF16),
            pltpu.VMEM((n, piece + 16, hd), BF16),
            pltpu.VMEM((n, piece, hd), BF16),
            pltpu.VMEM((owners, piece, hd), BF16),
            pltpu.VMEM((owners, piece, hd), BF16),
            pltpu.VMEM((n, piece, hd), BF16),
            pltpu.VMEM((n, piece, hd), BF16),
            pltpu.VMEM((owners, piece, hd), BF16),
            pltpu.VMEM((max(nt - 1, 1), rows_t, wide), BF16),
            pltpu.VMEM((max(nt - 1, 1), rows_t, wide), BF16),
            dma, dma, dma((nt,)), dma((nt,)),
            dma((n,)), dma((n,)), dma((n,)), dma((n,)),
            dma((n,)), dma((n,)), dma((n,)), dma((n,)),
            dma((nt,)), dma((nt,)),
        ],
        compiler_params=pltpu.CompilerParams(
            collective_id=0, has_side_effects=True, vmem_limit_bytes=58 * 1024 * 1024
        ),
        cost_estimate=cost,
    )(q, k, v, ld, sid.reshape(1, -1), gain.reshape(1, -1), w, cot)


def solution(mesh):
    n, nt = mesh.shape["tm"], mesh.shape["tensor"]
    return jax.shard_map(
        functools.partial(on_device, n, nt),
        mesh=mesh,
        in_specs=(
            P("tm", "tensor"),
            P("tm", "tensor"),
            P("tm", "tensor"),
            P("tensor", "tm"),
            P("tm"),
            P("tensor"),
            P("tensor", None),
            P(("tm", "tensor"), None),
        ),
        out_specs=(
            P(("tm", "tensor"), None),
            P("tm", "tensor"),
            P("tm", "tensor"),
            P("tm", "tensor"),
        ),
        check_vma=False,
    )
```

time: 314 us -> 56.7 us (0.18)
  waiting for transfers between devices: 179 us -> 0 us
  Pallas kernels: 0 us -> 48.4 us
  blocking collectives: 43.6 us -> 0 us
  matrix products: 40.4 us -> 0 us
  other arithmetic: 23.2 us -> 0 us
  between operations: 14.7 us -> 0.65 us
  local copies, waits for them, and re-layouts: 11 us -> 7.2 us
    all_gather x3 -> x0, waiting for transfers between devices: 178 us -> none  [the longest x2 178 us: entering(): gathered = jax.tree.map(lambda a: lax.all_gather(a, axis), part)]
    pallas_call x0 -> x1, Pallas kernels: none -> 48.4 us  [on_device(): pl.pallas_call(functools.partial(kernel, n, nt, owners), out_shape=(jax.S...]
    unnamed x1 -> x0, blocking collectives: 43.6 us -> none
    dot_general x14 -> x0, matrix products: 40.4 us -> none  [the longest x1 10 us: on_device(): lax.dot_general(lax.all_gather(out_cotangent, 'tensor', axis=0, tiled=Tru...]
    add x15 -> x0, other arithmetic: 18.2 us -> none  [chain_combine(): later[0][:, None, None] * earlier[1] + later[1]]
    unnamed x36 -> x10, local copies, waits for them, and re-layouts: 8.7 us -> 5.96 us
  transfers between devices with their start and end apart: 4 -> 0, of which waited for: 2 -> 0; matrix products, arithmetic and copies ran while one was open for 21% -> 0% of each run, Pallas kernels for 0% -> 0%
where the time goes in v1:
time: 56.7 us; the launch traced here: 56.3 us
  Pallas kernels  48.4 us (85%)
  local copies, waits for them, and re-layouts  7.2 us (13%)
  between operations  0.65 us (1%)
    pallas_call x1, Pallas kernels, on_device(): pl.pallas_call(functools.partial(kernel, n, nt, owners), out_shape=(jax.S...  48.4 us
    unnamed x10, local copies, waits for them, and re-layouts  5.96 us
    reshape x1, local copies, waits for them, and re-layouts, on_device(): sid.reshape(1, -1)  1.25 us

profile of v1, /device:TPU:0, one launch (start us, length us, event | category | flops | bytes accessed | tf_op | source)
XLA Modules:
  0.0 56.3 jit_solution(17347205413747372863)
XLA Ops:
  0.6 1.2 %reshape.14.sid_ref = s32[1,384]{1,0:T(1,128)} reshape(s32[384]{0:T(512)} %param.12) | data formatting | bytes 3072 | tf_op jit(solution)/shard_map/reshape | solution.py:399
  1.9 48.4 %shard_map.111 = (bf16[192,4096]{1,0:T(8,128)(2,1)}, bf16[384,1024]{1,0:T(8,128)(2,1)}, bf16[384,1024]{1,0:T(8,128)(2,1)}, bf16[384,1024]{1,0:T(8,128)(2,1)}) custom-call(bf16[384,1024]{1,0:T(8,128)(2,1)} %q_ref.1, bf16[384,1024]{1,0:T(8,128)(2,1)} %k_ref.1, bf16[384,1024]{1,0:T(8,128)(2,1)} %v_ref.1, f32[8,384]{1,0:T(8,128)} %ld_ref.1, ...), custom_call_target="tpu_custom_call" | custom-call | flops 9160359936 | bytes 14680064 | tf_op jit(solution)/shard_map/pallas_call | solution.py:358
  50.3 0.0 copy-start.2
  50.3 2.8 %copy.16 = bf16[192,4096]{1,0:T(8,128)(2,1)} copy(bf16[192,4096]{1,0:T(8,128)(2,1)} %get-tuple-element.8) | data formatting | bytes 3145728
  53.1 0.0 copy-done.2
  53.1 0.0 copy-start.1
  53.1 0.0 copy-start
  53.1 0.9 %copy.17 = bf16[384,1024]{1,0:T(8,128)(2,1)} copy(bf16[384,1024]{1,0:T(8,128)(2,1)S(1)} %copy-done.2) | data formatting | bytes 1572864
  54.0 0.5 copy-done.1
  54.5 0.9 %copy.18 = bf16[384,1024]{1,0:T(8,128)(2,1)} copy(bf16[384,1024]{1,0:T(8,128)(2,1)S(1)} %copy-done.1) | data formatting | bytes 1572864
  55.4 0.0 copy-done
  55.4 0.9 %copy.19 = bf16[384,1024]{1,0:T(8,128)(2,1)} copy(bf16[384,1024]{1,0:T(8,128)(2,1)S(1)} %copy-done) | data formatting | bytes 1572864
Async XLA Ops:
  50.3 2.8 %copy-start.2 = (bf16[384,1024]{1,0:T(8,128)(2,1)S(1)}, bf16[384,1024]{1,0:T(8,128)(2,1)}, u32[]{:S(2)}) copy-start(bf16[384,1024]{1,0:T(8,128)(2,1)} %get-tuple-element.9) | copy-start | bytes 2359300
  53.1 1.4 %copy-start.1 = (bf16[384,1024]{1,0:T(8,128)(2,1)S(1)}, bf16[384,1024]{1,0:T(8,128)(2,1)}, u32[]{:S(2)}) copy-start(bf16[384,1024]{1,0:T(8,128)(2,1)} %get-tuple-element.10) | copy-start | bytes 2359300
  53.1 2.3 %copy-start = (bf16[384,1024]{1,0:T(8,128)(2,1)S(1)}, bf16[384,1024]{1,0:T(8,128)(2,1)}, u32[]{:S(2)}) copy-start(bf16[384,1024]{1,0:T(8,128)(2,1)} %get-tuple-element.11) | copy-start | bytes 2359300

commit v2 on v1

v2 whole, which is shorter than its diff:
```python
import functools

import jax
import jax.numpy as jnp
from jax import lax
from jax.experimental import pallas as pl
from jax.experimental.pallas import tpu as pltpu
from jax.sharding import PartitionSpec as P

EPSILON = 1e-06
F32 = jnp.float32
BF16 = jnp.bfloat16
MESH = pl.DeviceIdType.MESH
NT = (((1,), (1,)), ((), ()))
TN = (((0,), (0,)), ((), ()))
NN = (((1,), (0,)), ((), ()))


def mm(a, b, dims, precision=None):
    return lax.dot_general(a, b, dims, precision=precision, preferred_element_type=F32)


def owners_of(rows, head_size, count):
    owners = count
    while rows % owners or (rows // owners) % 16 or head_size % (rows // owners):
        owners -= 1
    return owners


def kernel(
    n, nt, owners,
    ld_ref, sid_ref, gain_ref, q_hbm, k_hbm, v_hbm, w_hbm, cot_hbm,
    out_ref, qg_ref, kg_ref, vg_ref,
    q_ref, k_ref, v_ref, w, cot, bound, cumrow, kscale, ends, escale, decayed, weights, probs,
    local, outgrad, attended, mixgrad, vlocal, klocal, decays,
    send_s, recv_s, send_p, prefix, send_g, recv_g, send_l, later,
    send_t, recv_t, send_u, recv_u, part_o, recv_o,
    w_sem, cot_sem, q_sem, k_sem, v_sem, c_send, c_recv, s_send, s_recv, p_send, p_recv,
    g_send, g_recv, l_send, l_recv, o_send, o_recv, t_send, t_recv, u_send, u_recv,
):
    group = n // 2
    me = lax.axis_index("tm")
    my_t = lax.axis_index("tensor")
    upper = me >= group
    base = (me // group) * group
    place = me - base
    peer = lax.rem(me + group, n)
    tok = q_ref.shape[0]
    heads = ld_ref.shape[0]
    hd = q_ref.shape[1] // heads
    rows_t = tok // nt
    piece = heads * hd // owners
    per_head = owners // heads
    wide = w.shape[1]

    def other(k):
        return lax.rem(place + k, group)

    def source(k):
        return lax.rem(place + group - k, group)

    def owner_only(index, body):
        if owners == group:
            body()
        else:
            pl.when(index < owners)(body)

    def slot(index):
        return index if owners == group else jnp.minimum(index, owners - 1)

    def partners(body, lowest=1, count=group):
        def step(k, carry):
            body(k)
            return carry

        lax.fori_loop(lowest, count, step, 0)

    def some_heads(body, low, high):
        width = 2 if (high - low) % 2 == 0 else 1

        def step(i, carry):
            for u in range(width):
                h = low + i * width + u
                body(h, pl.ds(pl.multiple_of(h * hd, hd), hd))
            return carry

        lax.fori_loop(0, (high - low) // width, step, 0)

    barrier = pltpu.get_barrier_semaphore()
    partners(lambda k: pl.semaphore_signal(
        barrier, inc=1, device_id={"tm": base + other(k)}, device_id_type=MESH))
    pl.semaphore_signal(barrier, inc=1, device_id={"tm": peer}, device_id_type=MESH)
    partners(lambda k: pl.semaphore_signal(
        barrier, inc=1, device_id={"tensor": lax.rem(my_t + k, nt)}, device_id_type=MESH), 1, nt)

    k_copy = pltpu.make_async_copy(k_hbm, k_ref, k_sem)
    v_copy = pltpu.make_async_copy(v_hbm, v_ref, v_sem)
    q_copy = pltpu.make_async_copy(q_hbm, q_ref, q_sem)
    w_copy = pltpu.make_async_copy(w_hbm, w, w_sem)
    my_rows = pl.ds(pl.multiple_of(my_t * rows_t, 16), rows_t)
    cot_copy = pltpu.make_async_copy(cot_hbm, cot.at[my_rows], cot_sem)
    k_copy.start()
    v_copy.start()
    q_copy.start()
    w_copy.start()
    cot_copy.start()

    row_id = lax.broadcasted_iota(jnp.int32, (tok, tok), 0)
    col_id = lax.broadcasted_iota(jnp.int32, (tok, tok), 1)
    ld = ld_ref[...]
    highest = lax.Precision.HIGHEST
    tri = jnp.where(col_id <= row_id, 1.0, 0.0)
    cumcol = mm(tri, ld, NT, highest)
    top = lax.broadcasted_iota(jnp.int32, (16, hd), 0) < 8
    for h in range(heads):
        cum_h = cumcol[:, h : h + 1]
        end_h = cum_h[tok - 1 : tok]
        kscale[h] = jnp.broadcast_to(jnp.exp(end_h - cum_h), (tok, hd))
        g = jnp.broadcast_to(jnp.exp(end_h), (16, hd))
        high = g.astype(BF16).astype(F32)
        extra = jnp.where(top, high, g - high).astype(BF16)
        for r in range(per_head):
            send_s[h * per_head + r, piece:, :] = extra

    k_copy.wait()
    v_copy.wait()

    def state_step(h, cols):
        kp = jnp.maximum(k_ref[:, cols], 0).astype(F32)
        dec = (kscale[h] * kp).astype(BF16)
        decayed[:, cols] = dec
        state = mm(dec, v_ref[:, cols], TN).astype(BF16)
        for r in range(per_head):
            send_s[h * per_head + r, :piece, :] = state[r * piece : (r + 1) * piece]

    some_heads(state_step, 0, heads)
    pl.semaphore_wait(barrier, group + nt - 1)

    def to_owner(src, dst, ss, rs, k):
        return pltpu.make_async_remote_copy(
            src.at[slot(other(k))], dst.at[place], ss.at[k], rs.at[k],
            device_id={"tm": base + other(k)}, device_id_type=MESH)

    def from_any(src, dst, ss, rs, k):
        return pltpu.make_async_remote_copy(
            src.at[0], dst.at[source(k)], ss.at[k], rs.at[k],
            device_id={"tm": base + other(k)}, device_id_type=MESH)

    def to_any(src, dst, ss, rs, k):
        return pltpu.make_async_remote_copy(
            src.at[other(k)], dst.at[slot(place)], ss.at[k], rs.at[k],
            device_id={"tm": base + other(k)}, device_id_type=MESH)

    def from_owner(src, dst, ss, rs, k):
        return pltpu.make_async_remote_copy(
            src.at[0], dst.at[slot(source(k))], ss.at[k], rs.at[k],
            device_id={"tm": base + other(k)}, device_id_type=MESH)

    def gather_start(*way):
        partners(lambda k: owner_only(other(k), lambda: to_owner(*way, k).start()))

        def keep():
            way[1][place] = way[0][slot(place)]

        owner_only(place, keep)

    def gather_wait(*way):
        owner_only(place, lambda: partners(lambda k: from_any(*way, k).wait_recv()))

    def spread_start(*way):
        def go():
            partners(lambda k: to_any(*way, k).start())
            way[1][slot(place)] = way[0][place]

        owner_only(place, go)

    def spread_wait(*way):
        partners(lambda k: owner_only(source(k), lambda: from_owner(*way, k).wait_recv()))

    def sends_wait(way_g, way_s):
        partners(lambda k: owner_only(other(k), lambda: to_owner(*way_g, k).wait_send()))
        owner_only(place, lambda: partners(lambda k: to_any(*way_s, k).wait_send()))

    fwd_g = (send_s, recv_s, s_send, s_recv)
    fwd_s = (send_p, prefix, p_send, p_recv)
    bwd_g = (send_g, recv_g, g_send, g_recv)
    bwd_s = (send_l, later, l_send, l_recv)

    def total_copy(src, dst, ss, rs):
        return pltpu.make_async_remote_copy(
            src, dst, ss, rs, device_id={"tm": peer}, device_id_type=MESH)

    fwd_t = (send_t, recv_t, t_send, t_recv)
    bwd_t = (send_u, recv_u, u_send, u_recv)

    gather_start(*fwd_g)

    def cot_remote(k):
        return pltpu.make_async_remote_copy(
            cot_hbm, cot.at[my_rows], c_send.at[k], c_recv.at[k],
            device_id={"tensor": lax.rem(my_t + k, nt)}, device_id_type=MESH)

    def cot_arrival(k):
        s = lax.rem(my_t + nt - k, nt)
        return pltpu.make_async_remote_copy(
            cot_hbm, cot.at[pl.ds(pl.multiple_of(s * rows_t, 16), rows_t)],
            c_send.at[k], c_recv.at[k],
            device_id={"tensor": lax.rem(my_t + k, nt)}, device_id_type=MESH)

    partners(lambda k: cot_remote(k).start(), 1, nt)

    sid_row = jnp.broadcast_to(sid_ref[...].reshape(1, tok).astype(F32), (tok, tok))
    sid_col = jnp.sum(jnp.where(row_id == col_id, sid_row, 0.0), axis=1, keepdims=True)
    visible = sid_row <= sid_col
    bound[...] = jnp.where(visible, 0.0, -1e30)
    cumrow[...] = mm(ld, tri, NT, highest)
    cendcol = mm(jnp.where(visible, 1.0, 0.0), ld, NT, highest)
    for h in range(heads):
        end_b = jnp.broadcast_to(cendcol[:, h : h + 1], (tok, hd))
        ends[h] = end_b
        escale[h] = jnp.exp(end_b)
    q_copy.wait()

    def inner_step(h, cols):
        qp = jnp.maximum(q_ref[:, cols], 0)
        kp = jnp.maximum(k_ref[:, cols], 0)
        end = jnp.concatenate([ends[h]] * (tok // hd), axis=1)
        weight = jnp.exp(jnp.minimum(end - cumrow[pl.ds(h, 1), :], bound[...]))
        weights[h] = weight
        p = (weight * mm(qp, kp, NT)).astype(BF16)
        probs[h] = p
        local[:, cols] = mm(p, v_ref[:, cols], NN)

    half, most = heads // 2, 3 * heads // 4
    some_heads(inner_step, 0, half)

    gather_wait(*fwd_g)

    def scan_forward(state):
        def step(b, state):
            send_p[b] = state.astype(BF16)
            got = recv_s[b].astype(F32)
            g = got[piece : piece + 1] + got[piece + 8 : piece + 9]
            decays[pl.ds(b, 1), :] = g
            return g * state + got[:piece]

        return lax.fori_loop(0, group, step, state)

    def first_forward():
        def go():
            send_t[...] = scan_forward(jnp.zeros((piece, hd), F32)).astype(BF16)
            total_copy(*fwd_t).start()

        owner_only(place, go)
        spread_start(*fwd_s)

    def second_forward():
        def go():
            total_copy(*fwd_t).wait_recv()
            scan_forward(recv_t[...].astype(F32))

        owner_only(place, go)
        spread_start(*fwd_s)

    pl.when(jnp.logical_not(upper))(first_forward)
    some_heads(inner_step, half, most)
    pl.when(upper)(second_forward)
    some_heads(inner_step, most, heads)

    w_copy.wait()
    cot_copy.wait()
    partners(lambda k: cot_arrival(k).wait_recv(), 1, nt)
    chunk = 2 * hd if heads % 2 == 0 else hd

    def outgrad_step(c, carry):
        part = pl.ds(pl.multiple_of(c * chunk, chunk), chunk)
        outgrad[:, part] = mm(cot[...], w[part, :], NT)
        return carry

    lax.fori_loop(0, heads * hd // chunk, outgrad_step, 0)

    spread_wait(*fwd_s)

    def head_rows(buffer, h):
        parts = [buffer[h * per_head + r] for r in range(per_head)]
        return parts[0] if per_head == 1 else jnp.concatenate(parts, axis=0)

    def norm_step(h, cols):
        qp = jnp.maximum(q_ref[:, cols], 0)
        es = escale[h]
        mixed = local[:, cols] + es * mm(qp, head_rows(prefix, h), NN)
        inv = lax.rsqrt(jnp.mean(mixed * mixed, axis=1, keepdims=True) + EPSILON)
        gain = gain_ref[:, cols]
        attended[:, cols] = (mixed * inv * gain).astype(BF16)
        gained = outgrad[:, cols] * gain
        along = jnp.mean(mixed * gained, axis=1, keepdims=True)
        mg = (inv * gained - mixed * (inv * inv * inv * along)).astype(BF16)
        mixgrad[:, cols] = mg
        sq = (es * qp.astype(F32)).astype(BF16)
        grad = mm(sq, mg, TN).astype(BF16)
        for r in range(per_head):
            send_g[h * per_head + r] = grad[r * piece : (r + 1) * piece]

    some_heads(norm_step, 0, heads)
    gather_start(*bwd_g)

    step_cols = 512

    def project(c, carry):
        part = pl.ds(pl.multiple_of(c * step_cols, step_cols), step_cols)
        part_o[:, part] = mm(attended[...], w[:, part], NN).astype(BF16)
        return carry

    lax.fori_loop(0, wide // step_cols, project, 0)

    def out_copy(k):
        d = lax.rem(my_t + k, nt)
        return pltpu.make_async_remote_copy(
            part_o.at[pl.ds(pl.multiple_of(d * rows_t, 16), rows_t)], recv_o.at[k - 1],
            o_send.at[k], o_recv.at[k], device_id={"tensor": d}, device_id_type=MESH)

    partners(lambda k: out_copy(k).start(), 1, nt)

    gather_wait(*bwd_g)

    def scan_backward(state):
        def step(i, state):
            b = group - 1 - i
            send_l[b] = state.astype(BF16)
            return decays[pl.ds(b, 1), :] * state + recv_g[b].astype(F32)

        return lax.fori_loop(0, group, step, state)

    def first_backward():
        def go():
            send_u[...] = scan_backward(jnp.zeros((piece, hd), F32)).astype(BF16)
            total_copy(*bwd_t).start()

        owner_only(place, go)
        spread_start(*bwd_s)

    def second_backward():
        def go():
            total_copy(*bwd_t).wait_recv()
            scan_backward(recv_u[...].astype(F32))

        owner_only(place, go)
        spread_start(*bwd_s)

    def grad_step(h, cols):
        qp = jnp.maximum(q_ref[:, cols], 0)
        kp = jnp.maximum(k_ref[:, cols], 0)
        mg = mixgrad[:, cols]
        sg = (weights[h] * mm(mg, v_ref[:, cols], NT)).astype(BF16)
        vlocal[:, cols] = mm(probs[h], mg, TN)
        klocal[:, cols] = mm(sg, qp, TN)
        qg = mm(sg, kp, NN) + escale[h] * mm(mg, head_rows(prefix, h), NT)
        qg_ref[:, cols] = jnp.where(qp.astype(F32) > 0, qg, 0.0).astype(BF16)

    early = heads // 4
    pl.when(upper)(first_backward)
    some_heads(grad_step, 0, early)
    pl.when(jnp.logical_not(upper))(second_backward)
    some_heads(grad_step, early, heads)

    partners(lambda k: out_copy(k).wait_recv(), 1, nt)

    def total_out(c, carry):
        part = pl.ds(pl.multiple_of(c * step_cols, step_cols), step_cols)
        total = part_o[my_rows, part].astype(F32)
        for k in range(1, nt):
            total += recv_o[k - 1, :, part].astype(F32)
        out_ref[:, part] = total.astype(BF16)
        return carry

    lax.fori_loop(0, wide // step_cols, total_out, 0)

    spread_wait(*bwd_s)

    def last_step(h, cols):
        lat = head_rows(later, h)
        vg_ref[:, cols] = (vlocal[:, cols] + mm(decayed[:, cols], lat, NN)).astype(BF16)
        kg = klocal[:, cols] + kscale[h] * mm(v_ref[:, cols], lat, NT)
        kg_ref[:, cols] = jnp.where(k_ref[:, cols].astype(F32) > 0, kg, 0.0).astype(BF16)

    some_heads(last_step, 0, heads)

    partners(lambda k: cot_remote(k).wait_send(), 1, nt)
    partners(lambda k: out_copy(k).wait_send(), 1, nt)
    sends_wait(fwd_g, fwd_s)
    sends_wait(bwd_g, bwd_s)
    pl.when(jnp.logical_not(upper))(
        lambda: owner_only(place, lambda: total_copy(*fwd_t).wait_send()))
    pl.when(upper)(lambda: owner_only(place, lambda: total_copy(*bwd_t).wait_send()))


def write_kernel(*refs):
    count = (len(refs) - 1) // 2
    sems = refs[-1]
    copies = [
        pltpu.make_async_copy(refs[i], refs[count + i], sems.at[i]) for i in range(count)
    ]
    for copy in copies:
        copy.start()
    for copy in copies:
        copy.wait()


def on_device(n, nt, q, k, v, ld, sid, gain, w, cot):
    tok, width = q.shape
    heads = ld.shape[0]
    hd = width // heads
    wide = w.shape[1]
    rows_t = cot.shape[0]
    group = n // 2
    owners = owners_of(width, hd, group)
    piece = width // owners
    vmem = pl.BlockSpec(memory_space=pltpu.VMEM)
    hbm = pl.BlockSpec(memory_space=pl.ANY)
    dma = pltpu.SemaphoreType.DMA
    flat16 = pltpu.VMEM((tok, width), BF16)
    flat32 = pltpu.VMEM((tok, width), F32)
    wide_h = pltpu.VMEM((heads, tok, hd), F32)
    one = pltpu.VMEM((piece, hd), BF16)
    by_owner = pltpu.VMEM((owners, piece, hd), BF16)
    by_place = pltpu.VMEM((group, piece, hd), BF16)
    shapes = ((rows_t, wide), (tok, width), (tok, width), (tok, width))
    cost = pl.CostEstimate(
        flops=4 * tok * width * wide + 14 * tok * tok * width + 12 * tok * width * hd,
        bytes_accessed=2 * width * wide + 16 * tok * width,
        transcendentals=heads * tok * tok,
    )
    results = pl.pallas_call(
        functools.partial(kernel, n, nt, owners),
        out_shape=tuple(pltpu.VMEM(shape, BF16) for shape in shapes),
        in_specs=[vmem] * 3 + [hbm] * 5,
        out_specs=(vmem,) * 4,
        scratch_shapes=[
            flat16, flat16, flat16,
            pltpu.VMEM(w.shape, BF16),
            pltpu.VMEM((tok, wide), BF16),
            pltpu.VMEM((tok, tok), F32),
            pltpu.VMEM((heads, tok), F32),
            wide_h, wide_h, wide_h,
            flat16,
            pltpu.VMEM((heads, tok, tok), F32),
            pltpu.VMEM((heads, tok, tok), BF16),
            flat32, flat32, flat16, flat16, flat32, flat32,
            pltpu.VMEM((group, hd), F32),
            pltpu.VMEM((owners, piece + 16, hd), BF16),
            pltpu.VMEM((group, piece + 16, hd), BF16),
            by_place, by_owner, by_owner, by_place, by_place, by_owner,
            one, one, one, one,
            pltpu.VMEM((tok, wide), BF16),
            pltpu.VMEM((max(nt - 1, 1), rows_t, wide), BF16),
            dma, dma, dma, dma, dma, dma((nt,)), dma((nt,)),
            dma((group,)), dma((group,)), dma((group,)), dma((group,)),
            dma((group,)), dma((group,)), dma((group,)), dma((group,)),
            dma((nt,)), dma((nt,)), dma, dma, dma, dma,
        ],
        compiler_params=pltpu.CompilerParams(
            collective_id=0, has_side_effects=True, vmem_limit_bytes=50 * 1024 * 1024
        ),
        cost_estimate=cost,
    )(ld, sid, gain.reshape(1, -1), q, k, v, w, cot)
    return pl.pallas_call(
        write_kernel,
        out_shape=tuple(jax.ShapeDtypeStruct(shape, BF16) for shape in shapes),
        in_specs=[vmem] * 4,
        out_specs=(hbm,) * 4,
        scratch_shapes=[dma((4,))],
    )(*results)


def solution(mesh):
    n, nt = mesh.shape["tm"], mesh.shape["tensor"]
    return jax.shard_map(
        functools.partial(on_device, n, nt),
        mesh=mesh,
        in_specs=(
            P("tm", "tensor"),
            P("tm", "tensor"),
            P("tm", "tensor"),
            P("tensor", "tm"),
            P("tm"),
            P("tensor"),
            P("tensor", None),
            P(("tm", "tensor"), None),
        ),
        out_specs=(
            P(("tm", "tensor"), None),
            P("tm", "tensor"),
            P("tm", "tensor"),
            P("tm", "tensor"),
        ),
        check_vma=False,
    )
```

time: 56.7 us -> 47.6 us (0.84)
  Pallas kernels: 48.4 us -> 40.8 us
  local copies, waits for them, and re-layouts: 7.2 us -> 5.85 us
    pallas_call x1 -> x2, Pallas kernels: 48.4 us -> 40.8 us  [the longest x1 36.8 us: on_device(): pl.pallas_call(functools.partial(kernel, n, nt, owners), out_shape=tuple(...]
    reshape x1 -> x0, local copies, waits for them, and re-layouts: 1.25 us -> none  [on_device(): sid.reshape(1, -1)]
    unnamed x10 -> x14, local copies, waits for them, and re-layouts: 5.96 us -> 5.85 us
where the time goes in v2:
time: 47.6 us; the launch traced here: 47.4 us
  Pallas kernels  40.8 us (86%)
  local copies, waits for them, and re-layouts  5.85 us (12%)
  between operations  0.66 us (1%)
    pallas_call x1, Pallas kernels, on_device(): pl.pallas_call(functools.partial(kernel, n, nt, owners), out_shape=tuple(...  36.8 us
    unnamed x14, local copies, waits for them, and re-layouts  5.85 us
    pallas_call x1, Pallas kernels, on_device(): pl.pallas_call(write_kernel, out_shape=tuple((jax.ShapeDtypeStruct(shape,...  4.03 us

profile of v2, /device:TPU:0, one launch (start us, length us, event | category | flops | bytes accessed | tf_op | source)
XLA Modules:
  0.0 47.4 jit_solution(15116013346212985055)
XLA Ops:
  0.6 0.0 copy-start.4
  0.6 0.7 %copy-done.4 = f32[8,384]{1,0:T(8,128)S(1)} copy-done((f32[8,384]{1,0:T(8,128)S(1)}, f32[8,384]{1,0:T(8,128)}, u32[]{:S(2)}) %copy-start.4) | copy-done | bytes 12312
  1.3 0.0 copy-start.5
  1.3 0.7 %copy-done.5 = f32[1024]{0:T(1024)S(1)} copy-done((f32[1024]{0:T(1024)S(1)}, f32[1024]{0:T(1024)}, u32[]{:S(2)}) %copy-start.5) | copy-done | bytes 4120
  2.0 0.0 copy-start.6
  2.0 0.7 %copy-done.6 = s32[384]{0:T(512)S(1)} copy-done((s32[384]{0:T(512)S(1)}, s32[384]{0:T(512)}, u32[]{:S(2)}) %copy-start.6) | copy-done | bytes 1560
  2.7 36.8 %shard_map.111 = (bf16[192,4096]{1,0:T(8,128)(2,1)S(1)}, bf16[384,1024]{1,0:T(8,128)(2,1)S(1)}, bf16[384,1024]{1,0:T(8,128)(2,1)S(1)}, bf16[384,1024]{1,0:T(8,128)(2,1)S(1)}) custom-call(f32[8,384]{1,0:T(8,128)S(1)} %copy-done.4, s32[384]{0:T(512)S(1)} %copy-done.6, f32[1,1024]{1,0:T(1,128)S(1)} %bitcast.1, bf16[384,1024]{1,0:T(8,128)(2,1)} %q_hbm.1, ...), custom_call_target="tpu_custom_call" | custom-call | flops 9160359936 | bytes 14680064 | tf_op jit(solution)/shard_map/pallas_call | solution.py:433
  39.5 0.0 copy-start
  39.6 1.1 %copy-done = bf16[192,4096]{1,0:T(8,128)(2,1)} copy-done((bf16[192,4096]{1,0:T(8,128)(2,1)}, bf16[192,4096]{1,0:T(8,128)(2,1)S(1)}, u32[]{:S(2)}) %copy-start) | copy-done | bytes 1572888
  40.7 0.0 copy-start.1
  40.7 0.9 %copy-done.1 = bf16[384,1024]{1,0:T(8,128)(2,1)} copy-done((bf16[384,1024]{1,0:T(8,128)(2,1)}, bf16[384,1024]{1,0:T(8,128)(2,1)S(1)}, u32[]{:S(2)}) %copy-start.1) | copy-done | bytes 786456
  41.6 0.0 copy-start.2
  41.6 0.9 %copy-done.2 = bf16[384,1024]{1,0:T(8,128)(2,1)} copy-done((bf16[384,1024]{1,0:T(8,128)(2,1)}, bf16[384,1024]{1,0:T(8,128)(2,1)S(1)}, u32[]{:S(2)}) %copy-start.2) | copy-done | bytes 786456
  42.5 0.0 copy-start.3
  42.5 0.9 %copy-done.3 = bf16[384,1024]{1,0:T(8,128)(2,1)} copy-done((bf16[384,1024]{1,0:T(8,128)(2,1)}, bf16[384,1024]{1,0:T(8,128)(2,1)S(1)}, u32[]{:S(2)}) %copy-start.3) | copy-done | bytes 786456
  43.3 4.0 %shard_map.112 = (bf16[192,4096]{1,0:T(8,128)(2,1)}, bf16[384,1024]{1,0:T(8,128)(2,1)}, bf16[384,1024]{1,0:T(8,128)(2,1)}, bf16[384,1024]{1,0:T(8,128)(2,1)}) custom-call(bf16[192,4096]{1,0:T(8,128)(2,1)} %copy-done, bf16[384,1024]{1,0:T(8,128)(2,1)} %copy-done.1, bf16[384,1024]{1,0:T(8,128)(2,1)} %copy-done.2, bf16[384,1024]{1,0:T(8,128)(2,1)} %copy-done.3), custom_call_target="tpu_custom_call" | custom-call | tf_op jit(solution)/shard_map/pallas_call | solution.py:466
Async XLA Ops:
  0.6 0.7 %copy-start.4 = (f32[8,384]{1,0:T(8,128)S(1)}, f32[8,384]{1,0:T(8,128)}, u32[]{:S(2)}) copy-start(f32[8,384]{1,0:T(8,128)} %ld_ref.1) | copy-start | bytes 36868
  1.3 0.7 %copy-start.5 = (f32[1024]{0:T(1024)S(1)}, f32[1024]{0:T(1024)}, u32[]{:S(2)}) copy-start(f32[1024]{0:T(1024)} %param.13) | copy-start | bytes 12292
  2.0 0.7 %copy-start.6 = (s32[384]{0:T(512)S(1)}, s32[384]{0:T(512)}, u32[]{:S(2)}) copy-start(s32[384]{0:T(512)} %sid_ref.1) | copy-start | bytes 4612
  39.5 1.1 %copy-start = (bf16[192,4096]{1,0:T(8,128)(2,1)}, bf16[192,4096]{1,0:T(8,128)(2,1)S(1)}, u32[]{:S(2)}) copy-start(bf16[192,4096]{1,0:T(8,128)(2,1)S(1)} %get-tuple-element.8.refs_0_) | copy-start | bytes 4718596
  40.7 0.9 %copy-start.1 = (bf16[384,1024]{1,0:T(8,128)(2,1)}, bf16[384,1024]{1,0:T(8,128)(2,1)S(1)}, u32[]{:S(2)}) copy-start(bf16[384,1024]{1,0:T(8,128)(2,1)S(1)} %get-tuple-element.9.refs_1_) | copy-start | bytes 2359300
  41.6 0.9 %copy-start.2 = (bf16[384,1024]{1,0:T(8,128)(2,1)}, bf16[384,1024]{1,0:T(8,128)(2,1)S(1)}, u32[]{:S(2)}) copy-start(bf16[384,1024]{1,0:T(8,128)(2,1)S(1)} %get-tuple-element.10.refs_2_) | copy-start | bytes 2359300
  42.5 0.9 %copy-start.3 = (bf16[384,1024]{1,0:T(8,128)(2,1)}, bf16[384,1024]{1,0:T(8,128)(2,1)S(1)}, u32[]{:S(2)}) copy-start(bf16[384,1024]{1,0:T(8,128)(2,1)S(1)} %get-tuple-element.11.refs_3_) | copy-start | bytes 2359300

commit v3 on v2

--- a/solution.py
+++ b/solution.py
@@ -29,13 +29,13 @@
 
 def kernel(
     n, nt, owners,
-    ld_ref, sid_ref, gain_ref, q_hbm, k_hbm, v_hbm, w_hbm, cot_hbm,
+    ld_hbm, sid_hbm, gain_hbm, q_hbm, k_hbm, v_hbm, w_hbm, cot_hbm,
     out_ref, qg_ref, kg_ref, vg_ref,
-    q_ref, k_ref, v_ref, w, cot, bound, cumrow, kscale, ends, escale, decayed, weights, probs,
+    ld_ref, sid_ref, gain_ref, q_ref, k_ref, v_ref, w, cot, bound, cumrow, kscale, ends, escale, decayed, weights, probs,
     local, outgrad, attended, mixgrad, vlocal, klocal, decays,
     send_s, recv_s, send_p, prefix, send_g, recv_g, send_l, later,
     send_t, recv_t, send_u, recv_u, part_o, recv_o,
-    w_sem, cot_sem, q_sem, k_sem, v_sem, c_send, c_recv, s_send, s_recv, p_send, p_recv,
+    small_sem, w_sem, cot_sem, q_sem, k_sem, v_sem, c_send, c_recv, s_send, s_recv, p_send, p_recv,
     g_send, g_recv, l_send, l_recv, o_send, o_recv, t_send, t_recv, u_send, u_recv,
 ):
     group = n // 2
@@ -52,6 +52,7 @@
     piece = heads * hd // owners
     per_head = owners // heads
     wide = w.shape[1]
+    direct = owners == group and per_head == 1 and group % 2 == 0
 
     def other(k):
         return lax.rem(place + k, group)
@@ -93,6 +94,12 @@
     partners(lambda k: pl.semaphore_signal(
         barrier, inc=1, device_id={"tensor": lax.rem(my_t + k, nt)}, device_id_type=MESH), 1, nt)
 
+    small = [
+        pltpu.make_async_copy(src, dst, small_sem.at[i])
+        for i, (src, dst) in enumerate(
+            ((ld_hbm, ld_ref), (sid_hbm, sid_ref), (gain_hbm, gain_ref)))
+    ]
+    small[0].start()
     k_copy = pltpu.make_async_copy(k_hbm, k_ref, k_sem)
     v_copy = pltpu.make_async_copy(v_hbm, v_ref, v_sem)
     q_copy = pltpu.make_async_copy(q_hbm, q_ref, q_sem)
@@ -101,15 +108,18 @@
     cot_copy = pltpu.make_async_copy(cot_hbm, cot.at[my_rows], cot_sem)
     k_copy.start()
     v_copy.start()
+    small[1].start()
+    small[2].start()
     q_copy.start()
     w_copy.start()
     cot_copy.start()
 
     row_id = lax.broadcasted_iota(jnp.int32, (tok, tok), 0)
     col_id = lax.broadcasted_iota(jnp.int32, (tok, tok), 1)
-    ld = ld_ref[...]
     highest = lax.Precision.HIGHEST
     tri = jnp.where(col_id <= row_id, 1.0, 0.0)
+    small[0].wait()
+    ld = ld_ref[...]
     cumcol = mm(tri, ld, NT, highest)
     top = lax.broadcasted_iota(jnp.int32, (16, hd), 0) < 8
     for h in range(heads):
@@ -133,7 +143,8 @@
         for r in range(per_head):
             send_s[h * per_head + r, :piece, :] = state[r * piece : (r + 1) * piece]
 
-    some_heads(state_step, 0, heads)
+    if not direct:
+        some_heads(state_step, 0, heads)
     pl.semaphore_wait(barrier, group + nt - 1)
 
     def to_owner(src, dst, ss, rs, k):
@@ -193,7 +204,28 @@
     fwd_t = (send_t, recv_t, t_send, t_recv)
     bwd_t = (send_u, recv_u, u_send, u_recv)
 
-    gather_start(*fwd_g)
+    def columns(h):
+        return pl.ds(pl.multiple_of(h * hd, hd), hd)
+
+    def keep_mine(src, dst, *_):
+        dst[place] = src[place]
+
+    if direct:
+        def state_pair(i, carry):
+            k = 2 * i + 1
+            state_step(other(k), columns(other(k)))
+            state_step(other(k + 1), columns(other(k + 1)))
+            to_owner(*fwd_g, k).start()
+            to_owner(*fwd_g, k + 1).start()
+            return carry
+
+        lax.fori_loop(0, group // 2 - 1, state_pair, 0)
+        state_step(other(group - 1), columns(other(group - 1)))
+        state_step(place, columns(place))
+        to_owner(*fwd_g, group - 1).start()
+        keep_mine(*fwd_g)
+    else:
+        gather_start(*fwd_g)
 
     def cot_remote(k):
         return pltpu.make_async_remote_copy(
@@ -209,6 +241,8 @@
 
     partners(lambda k: cot_remote(k).start(), 1, nt)
 
+    small[1].wait()
+    small[2].wait()
     sid_row = jnp.broadcast_to(sid_ref[...].reshape(1, tok).astype(F32), (tok, tok))
     sid_col = jnp.sum(jnp.where(row_id == col_id, sid_row, 0.0), axis=1, keepdims=True)
     visible = sid_row <= sid_col
@@ -231,7 +265,7 @@
         probs[h] = p
         local[:, cols] = mm(p, v_ref[:, cols], NN)
 
-    half, most = heads // 2, 3 * heads // 4
+    half, most = heads // 4, 3 * heads // 4
     some_heads(inner_step, 0, half)
 
     gather_wait(*fwd_g)
@@ -278,8 +312,6 @@
         return carry
 
     lax.fori_loop(0, heads * hd // chunk, outgrad_step, 0)
-
-    spread_wait(*fwd_s)
 
     def head_rows(buffer, h):
         parts = [buffer[h * per_head + r] for r in range(per_head)]
@@ -301,8 +333,28 @@
         for r in range(per_head):
             send_g[h * per_head + r] = grad[r * piece : (r + 1) * piece]
 
-    some_heads(norm_step, 0, heads)
-    gather_start(*bwd_g)
+    if direct:
+        norm_step(place, columns(place))
+        from_owner(*fwd_s, 1).wait_recv()
+        norm_step(source(1), columns(source(1)))
+        to_owner(*bwd_g, group - 1).start()
+
+        def norm_pair(i, carry):
+            k = 2 * i
+            from_owner(*fwd_s, k).wait_recv()
+            from_owner(*fwd_s, k + 1).wait_recv()
+            norm_step(source(k), columns(source(k)))
+            norm_step(source(k + 1), columns(source(k + 1)))
+            to_owner(*bwd_g, group - k).start()
+            to_owner(*bwd_g, group - k - 1).start()
+            return carry
+
+        lax.fori_loop(1, group // 2, norm_pair, 0)
+        keep_mine(*bwd_g)
+    else:
+        spread_wait(*fwd_s)
+        some_heads(norm_step, 0, heads)
+        gather_start(*bwd_g)
 
     step_cols = 512
 
@@ -311,15 +363,14 @@
         part_o[:, part] = mm(attended[...], w[:, part], NN).astype(BF16)
         return carry
 
-    lax.fori_loop(0, wide // step_cols, project, 0)
+    half_cols = wide // step_cols // 2
+    lax.fori_loop(0, half_cols, project, 0)
 
     def out_copy(k):
         d = lax.rem(my_t + k, nt)
         return pltpu.make_async_remote_copy(
             part_o.at[pl.ds(pl.multiple_of(d * rows_t, 16), rows_t)], recv_o.at[k - 1],
             o_send.at[k], o_recv.at[k], device_id={"tensor": d}, device_id_type=MESH)
-
-    partners(lambda k: out_copy(k).start(), 1, nt)
 
     gather_wait(*bwd_g)
 
@@ -357,8 +408,10 @@
         qg = mm(sg, kp, NN) + escale[h] * mm(mg, head_rows(prefix, h), NT)
         qg_ref[:, cols] = jnp.where(qp.astype(F32) > 0, qg, 0.0).astype(BF16)
 
-    early = heads // 4
+    early = heads // 2
     pl.when(upper)(first_backward)
+    lax.fori_loop(half_cols, wide // step_cols, project, 0)
+    partners(lambda k: out_copy(k).start(), 1, nt)
     some_heads(grad_step, 0, early)
     pl.when(jnp.logical_not(upper))(second_backward)
     some_heads(grad_step, early, heads)
@@ -375,15 +428,29 @@
 
     lax.fori_loop(0, wide // step_cols, total_out, 0)
 
-    spread_wait(*bwd_s)
-
     def last_step(h, cols):
         lat = head_rows(later, h)
         vg_ref[:, cols] = (vlocal[:, cols] + mm(decayed[:, cols], lat, NN)).astype(BF16)
         kg = klocal[:, cols] + kscale[h] * mm(v_ref[:, cols], lat, NT)
         kg_ref[:, cols] = jnp.where(k_ref[:, cols].astype(F32) > 0, kg, 0.0).astype(BF16)
 
-    some_heads(last_step, 0, heads)
+    if direct:
+        last_step(place, columns(place))
+        from_owner(*bwd_s, 1).wait_recv()
+        last_step(source(1), columns(source(1)))
+
+        def last_pair(i, carry):
+            k = 2 * i
+            from_owner(*bwd_s, k).wait_recv()
+            from_owner(*bwd_s, k + 1).wait_recv()
+            last_step(source(k), columns(source(k)))
+            last_step(source(k + 1), columns(source(k + 1)))
+            return carry
+
+        lax.fori_loop(1, group // 2, last_pair, 0)
+    else:
+        spread_wait(*bwd_s)
+        some_heads(last_step, 0, heads)
 
     partners(lambda k: cot_remote(k).wait_send(), 1, nt)
     partners(lambda k: out_copy(k).wait_send(), 1, nt)
@@ -430,12 +497,19 @@
         bytes_accessed=2 * width * wide + 16 * tok * width,
         transcendentals=heads * tok * tok,
     )
+    args = [
+        pltpu.with_memory_space_constraint(x, pltpu.HBM)
+        for x in (ld, sid, gain.reshape(1, -1), q, k, v, w, cot)
+    ]
     results = pl.pallas_call(
         functools.partial(kernel, n, nt, owners),
         out_shape=tuple(pltpu.VMEM(shape, BF16) for shape in shapes),
-        in_specs=[vmem] * 3 + [hbm] * 5,
+        in_specs=[pl.BlockSpec(memory_space=pltpu.HBM)] * 8,
         out_specs=(vmem,) * 4,
         scratch_shapes=[
+            pltpu.VMEM(ld.shape, F32),
+            pltpu.VMEM(sid.shape, jnp.int32),
+            pltpu.VMEM((1, width), F32),
             flat16, flat16, flat16,
             pltpu.VMEM(w.shape, BF16),
             pltpu.VMEM((tok, wide), BF16),
@@ -453,7 +527,7 @@
             one, one, one, one,
             pltpu.VMEM((tok, wide), BF16),
             pltpu.VMEM((max(nt - 1, 1), rows_t, wide), BF16),
-            dma, dma, dma, dma, dma, dma((nt,)), dma((nt,)),
+            dma((3,)), dma, dma, dma, dma, dma, dma((nt,)), dma((nt,)),
             dma((group,)), dma((group,)), dma((group,)), dma((group,)),
             dma((group,)), dma((group,)), dma((group,)), dma((group,)),
             dma((nt,)), dma((nt,)), dma, dma, dma, dma,
@@ -462,13 +536,14 @@
             collective_id=0, has_side_effects=True, vmem_limit_bytes=50 * 1024 * 1024
         ),
         cost_estimate=cost,
-    )(ld, sid, gain.reshape(1, -1), q, k, v, w, cot)
+    )(*args)
     return pl.pallas_call(
         write_kernel,
         out_shape=tuple(jax.ShapeDtypeStruct(shape, BF16) for shape in shapes),
-        in_specs=[vmem] * 4,
+        in_specs=[hbm] * 4,
         out_specs=(hbm,) * 4,
         scratch_shapes=[dma((4,))],
+        compiler_params=pltpu.CompilerParams(vmem_limit_bytes=2 * 1024 * 1024),
     )(*results)
 
 

time: 47.6 us -> 38.6 us (0.81)
  local copies, waits for them, and re-layouts: 5.85 us -> 0 us
  Pallas kernels: 40.8 us -> 37.8 us
    unnamed x14 -> x0, local copies, waits for them, and re-layouts: 5.85 us -> none
    pallas_call x1, Pallas kernels: 4.03 us -> 1.95 us  [on_device(): pl.pallas_call(write_kernel, out_shape=tuple((jax.ShapeDtypeStruct(shape,...]
    pallas_call x1, Pallas kernels: 36.8 us -> 35.8 us  [on_device(): pl.pallas_call(functools.partial(kernel, n, nt, owners), out_shape=tuple(...]
where the time goes in v3:
time: 38.6 us; the launch traced here: 38.4 us
  Pallas kernels  37.8 us (98%)
  between operations  0.64 us (2%)
    pallas_call x1, Pallas kernels, on_device(): pl.pallas_call(functools.partial(kernel, n, nt, owners), out_shape=tuple(...  35.8 us
    pallas_call x1, Pallas kernels, on_device(): pl.pallas_call(write_kernel, out_shape=tuple((jax.ShapeDtypeStruct(shape,...  1.95 us

profile of v3, /device:TPU:0, one launch (start us, length us, event | category | flops | bytes accessed | tf_op | source)
XLA Modules:
  0.0 38.4 jit_solution(12766917223410552252)
XLA Ops:
  0.6 35.8 %shard_map.111 = (bf16[192,4096]{1,0:T(8,128)(2,1)S(1)}, bf16[384,1024]{1,0:T(8,128)(2,1)S(1)}, bf16[384,1024]{1,0:T(8,128)(2,1)S(1)}, bf16[384,1024]{1,0:T(8,128)(2,1)S(1)}) custom-call(f32[8,384]{1,0:T(8,128)} %ld_hbm.1, s32[384]{0:T(512)} %sid_hbm.1, f32[1,1024]{1,0:T(1,128)} %bitcast.1, bf16[384,1024]{1,0:T(8,128)(2,1)} %q_hbm.1, ...), custom_call_target="tpu_custom_call" | custom-call | flops 9160359936 | bytes 14680064 | tf_op jit(solution)/shard_map/pallas_call | solution.py:504
  36.4 2.0 %shard_map.112 = (bf16[192,4096]{1,0:T(8,128)(2,1)}, bf16[384,1024]{1,0:T(8,128)(2,1)}, bf16[384,1024]{1,0:T(8,128)(2,1)}, bf16[384,1024]{1,0:T(8,128)(2,1)}) custom-call(bf16[192,4096]{1,0:T(8,128)(2,1)S(1)} %get-tuple-element.8.refs_0_, bf16[384,1024]{1,0:T(8,128)(2,1)S(1)} %get-tuple-element.9.refs_1_, bf16[384,1024]{1,0:T(8,128)(2,1)S(1)} %get-tuple-element.10.refs_2_, ...), custom_call_target="tpu_custom_call" | custom-call | tf_op jit(solution)/shard_map/pallas_call | solution.py:540

commit v4 on v3

--- a/solution.py
+++ b/solution.py
@@ -77,7 +77,7 @@
         lax.fori_loop(lowest, count, step, 0)
 
     def some_heads(body, low, high):
-        width = 2 if (high - low) % 2 == 0 else 1
+        width = next(size for size in (4, 2, 1) if (high - low) % size == 0)
 
         def step(i, carry):
             for u in range(width):
@@ -265,7 +265,7 @@
         probs[h] = p
         local[:, cols] = mm(p, v_ref[:, cols], NN)
 
-    half, most = heads // 4, 3 * heads // 4
+    half, most = heads // 2, heads // 2 + heads // 4
     some_heads(inner_step, 0, half)
 
     gather_wait(*fwd_g)

time: 38.6 us -> 38.8 us (level)
  no operation moved by 1% of the time
where the time goes in v4:
time: 38.8 us; the launch traced here: 38.6 us
  Pallas kernels  37.8 us (97%)
  between operations  0.8 us (2%)
    pallas_call x1, Pallas kernels, on_device(): pl.pallas_call(functools.partial(kernel, n, nt, owners), out_shape=tuple(...  35.8 us
    pallas_call x1, Pallas kernels, on_device(): pl.pallas_call(write_kernel, out_shape=tuple((jax.ShapeDtypeStruct(shape,...  1.95 us

profile of v4, /device:TPU:0, one launch (start us, length us, event | category | flops | bytes accessed | tf_op | source)
XLA Modules:
  0.0 38.6 jit_solution(1693638763315639822)
XLA Ops:
  0.6 35.8 %shard_map.111 = (bf16[192,4096]{1,0:T(8,128)(2,1)S(1)}, bf16[384,1024]{1,0:T(8,128)(2,1)S(1)}, bf16[384,1024]{1,0:T(8,128)(2,1)S(1)}, bf16[384,1024]{1,0:T(8,128)(2,1)S(1)}) custom-call(f32[8,384]{1,0:T(8,128)} %ld_hbm.1, s32[384]{0:T(512)} %sid_hbm.1, f32[1,1024]{1,0:T(1,128)} %bitcast.1, bf16[384,1024]{1,0:T(8,128)(2,1)} %q_hbm.1, ...), custom_call_target="tpu_custom_call" | custom-call | flops 9160359936 | bytes 14680064 | tf_op jit(solution)/shard_map/pallas_call | solution.py:504
  36.5 2.0 %shard_map.112 = (bf16[192,4096]{1,0:T(8,128)(2,1)}, bf16[384,1024]{1,0:T(8,128)(2,1)}, bf16[384,1024]{1,0:T(8,128)(2,1)}, bf16[384,1024]{1,0:T(8,128)(2,1)}) custom-call(bf16[192,4096]{1,0:T(8,128)(2,1)S(1)} %get-tuple-element.8.refs_0_, bf16[384,1024]{1,0:T(8,128)(2,1)S(1)} %get-tuple-element.9.refs_1_, bf16[384,1024]{1,0:T(8,128)(2,1)S(1)} %get-tuple-element.10.refs_2_, ...), custom_call_target="tpu_custom_call" | custom-call | tf_op jit(solution)/shard_map/pallas_call | solution.py:540
